TPU v7x, 32 devices: a whole 2x2x4 slice. The times are simulated.
32 devices in a mesh: traj: 8 (over z, y), mstate: 4 (over x, core).
Axes of the slice: x: 2, y: 2, z: 4, core: 2. Of those that a mesh axis runs over, the one named last changes fastest.
Arguments:
- bias: float32 [32, 262144], P(None, ('traj', 'mstate')), may hold values from -206 to 206
- labels: int32 [262144], P(('traj', 'mstate')), may hold values from 0 to 4095, as said below
- therm_index: int32 [262144], P(('traj', 'mstate')), may hold values from 0 to 31
- counts: int32 [32, 4096, 4096], P(None, 'traj', 'mstate'), may hold values from 0 to 4, as said below
- free_start: float32 [32, 4096], replicated, may hold values from -6 to 6
- mult_start: float32 [32, 4096], replicated, may hold values from -6 to 6
Outputs:
- free_energy: float32 [32, 4096], P(None, 'mstate')
- log_mult: float32 [32, 4096], P(None, 'mstate')
Inputs may be any that keep to these rules, and one draw needn't show every extreme that they name: `labels`: every Markov state is the label of at least one frame. `counts`: most entries are zero.
All inputs are finite; a program needn't handle non-finite values.
Results may differ from a plain program's by a relative error of at most 0.0001.
Values sent between devices are 32-bit elements; how exact they have to be, the bound alone decides.
A program may use at most 128 MiB of HBM per device.

v0:
```python
import jax
import jax.numpy as jnp
from jax import lax
from jax.sharding import PartitionSpec as P

ITERS = 2


def per_device(bias, labels, therm_index, counts, free_start, mult_start):
    states_k = bias.shape[0]
    width = free_start.shape[1]
    col_count = counts.shape[1]
    row_count = counts.shape[2]
    col_start = lax.axis_index("traj") * col_count
    row_start = lax.axis_index("mstate") * row_count
    states = jax.nn.one_hot(therm_index, states_k, dtype=jnp.float32)
    local_visits = jax.ops.segment_sum(states, labels, num_segments=width).T
    visits = lax.psum(local_visits, ("traj", "mstate"))
    counts_real = counts.astype(jnp.float32)
    free, mult = (free_start, mult_start)
    for step in range(ITERS):
        free_cols = lax.dynamic_slice_in_dim(free, col_start, col_count, 1)
        mult_cols = lax.dynamic_slice_in_dim(mult, col_start, col_count, 1)
        free_rows = lax.dynamic_slice_in_dim(free, row_start, row_count, 1)
        mult_rows = lax.dynamic_slice_in_dim(mult, row_start, row_count, 1)
        weight = jax.nn.sigmoid(
            mult_rows[:, None, :]
            + free_cols[:, :, None]
            - mult_cols[:, :, None]
            - free_rows[:, None, :]
        )
        partial_rows = jnp.sum(counts_real * weight, axis=1)
        row_total = lax.psum(partial_rows, "traj")
        mult = lax.all_gather(jnp.log(0.5 + row_total), "mstate", axis=1, tiled=True)
        level = jnp.log(jnp.exp(mult) + visits) + free
        scores = jnp.take(level, labels, axis=1) - bias
        top = jnp.max(scores, axis=0)
        logl = top + jnp.log(jnp.sum(jnp.exp(scores - top[None, :]), axis=0))
        term = -bias - logl[None, :]
        shift = lax.pmax(jnp.max(term, axis=1), ("traj", "mstate"))
        weights = jnp.exp(term - shift[:, None])
        local_total = jax.ops.segment_sum(weights.T, labels, num_segments=width).T
        total = lax.psum(local_total, ("traj", "mstate"))
        free = -(shift[:, None] + jnp.log(total))
    free_out = lax.dynamic_slice_in_dim(free, row_start, row_count, 1)
    mult_out = lax.dynamic_slice_in_dim(mult, row_start, row_count, 1)
    return (free_out, mult_out)


def solution(mesh):
    placed = (
        P(None, ("traj", "mstate")),
        P(("traj", "mstate")),
        P(("traj", "mstate")),
        P(None, "traj", "mstate"),
        P(),
        P(),
    )
    return jax.shard_map(
        per_device,
        mesh=mesh,
        in_specs=placed,
        out_specs=(P(None, "mstate"), P(None, "mstate")),
        check_vma=False,
    )
```

profile of v0, /device:TPU:0, one launch (start us, length us, event | category | flops | bytes accessed | tf_op | source)
XLA Modules:
  0.0 880.4 jit_solution(923992231987105623)
XLA Ops:
  7.2 0.0 all-reduce.6.cloned.1.call-start
  7.2 0.9 constant_dynamic-slice_fusion.6
  8.1 1.0 constant_dynamic-slice_fusion.5
  9.1 0.0 copy-start.10
  9.1 0.0 copy-start.11
  9.1 28.3 %multiply_reduce_fusion.1 = f32[32,1024]{1,0:T(8,128)} fusion(s32[32,512,1024]{2,1,0:T(8,128)} %param.11, f32[32,1024]{1,0:T(8,128)S(1)} %get-tuple-element.11, f32[32,512]{1,0:T(8,128)S(1)} %get-tuple-element.13, f32[32,512]{1,0:T(8,128)S(1)} %get-tuple-element.14, f32[32,1024]{1,0:T(8,128)S(1)} %get-tuple-element.12), kind=kLoop, calls=%fused_computation.6 | loop fusion | flops 150962176 | bytes 67633152 | tf_op jit(solution)/shard_map/reduce_sum | solution.py:32
  37.4 0.0 all-reduce.6.cloned.1.call-update
  37.4 0.0 all-reduce.8.cloned.1.call-start
  37.5 0.0 copy-done.10
  37.5 0.0 copy-done.11
  37.5 48.6 %scatter_custom_fusion = f32[4096,32]{1,0:T(8,128)S(1)} fusion(s32[8192]{0:T(1024)S(1)} %copy-done.10, s32[8192]{0:T(1024)S(1)} %copy-done.11, f32[]{:T(128)} %constant.11.clone.1), kind=kCustom, calls=%fused_computation.11 | custom fusion | flops 786432 | bytes 557060 | tf_op jit(solution)/shard_map/scatter-add | solution.py:17
  86.1 1.4 copy.42
  87.5 0.0 all-reduce.8.cloned.1.call-update
  87.5 0.0 all-reduce.10.cloned.1.call-start
  87.6 0.0 copy-done.2
  87.6 2.6 copy.44
  90.2 19.7 %all-reduce.6.cloned.1.call-done = f32[32,1024]{1,0:T(8,128)} async-done(((f32[32,1024]{1,0:T(8,128)}), f32[32,1024]{1,0:T(8,128)}) %all-reduce.6.cloned.1.call-update) | async-done | bytes 131088 | tf_op jit(solution)/shard_map/psum | solution.py:33
  109.9 0.9 add_log_fusion.1
  110.8 7.1 all_gather.6
  118.0 125.2 %all-reduce.8.cloned.1.call-done = f32[32,4096]{1,0:T(8,128)} async-done(((f32[32,4096]{1,0:T(8,128)}), f32[32,4096]{1,0:T(8,128)}) %all-reduce.8.cloned.1.call-update) | async-done | bytes 524304 | tf_op jit(solution)/shard_map/psum | solution.py:18
  243.2 0.0 copy-done.5
  243.2 0.0 copy-done.9
  243.2 2.0 log_add_fusion.1
  245.1 1.6 copy.43
  246.8 27.7 %gather_fusion = f32[8192,32]{1,0:T(8,128)} fusion(f32[32,4096]{0,1:T(8,128)S(1)} %copy.43, s32[8192]{0:T(1024)S(1)} %fusion.12), kind=kCustom, calls=%fused_computation.clone | custom fusion | bytes 2129920 | tf_op jit(solution)/shard_map/jit(_take)/gather | solution.py:36
  274.5 6.5 fusion.8
  281.1 0.0 copy-done
  281.1 4.0 exponential_reduce_fusion.1
  285.1 0.2 subtract_reduce_fusion.1
  285.3 39.2 %pmax.14 = f32[32]{0:T(128)S(1)} all-reduce(f32[32]{0:T(128)S(1)} %subtract_reduce_fusion.1), channel_id=1, replica_groups=mesh['traj'=8,'mstate'=4] {'traj','mstate'}, use_global_device_ids=true, to_apply=%region_7.9 | all-reduce | flops 32 | bytes 256 | tf_op jit(solution)/shard_map/pmax | solution.py:40
  324.6 0.2 exponential_bitcast_fusion.1
  324.8 2.7 copy.45
  327.4 44.8 %scatter_custom_fusion.1 = f32[4096,32]{1,0:T(8,128)S(1)} fusion(s32[8192]{0:T(1024)S(1)} %copy-done.10, f32[8192,32]{1,0:T(8,128)} %copy.45, f32[]{:T(128)} %constant.11.clone.1), kind=kCustom, calls=%fused_computation.19 | custom fusion | flops 262144 | bytes 524800 | tf_op jit(solution)/shard_map/scatter-add | solution.py:42
  372.3 1.4 copy.46
  373.7 0.0 all-reduce.10.cloned.1.call-update
  373.7 0.2 all-reduce.12.cloned.1.call-start
  373.9 0.9 constant_dynamic-slice_fusion.2
  374.8 0.9 constant_dynamic-slice_fusion.4
  375.7 125.9 %all-reduce.10.cloned.1.call-done = f32[32,4096]{1,0:T(8,128)} async-done(((f32[32,4096]{1,0:T(8,128)}), f32[32,4096]{1,0:T(8,128)}) %all-reduce.10.cloned.1.call-update) | async-done | bytes 524304 | tf_op jit(solution)/shard_map/psum | solution.py:43
  501.6 1.2 add_negate_fusion
  502.8 28.3 %multiply_reduce_fusion = f32[32,1024]{1,0:T(8,128)} fusion(s32[32,512,1024]{2,1,0:T(8,128)} %param.11, f32[32,1024]{1,0:T(8,128)S(1)} %constant_dynamic-slice_fusion.1, f32[32,512]{1,0:T(8,128)S(1)} %constant_dynamic-slice_fusion.2, f32[32,512]{1,0:T(8,128)S(1)} %constant_dynamic-slice_fusion.3, f32[32,1024]{1,0:T(8,128)S(1)} %constant_dynamic-slice_fusion.4), kind=kLoop, calls=%fused_computation.5 | loop fusion | flops 150962176 | bytes 67633152 | tf_op jit(solution)/shard_map/reduce_sum | solution.py:32
  531.1 0.0 all-reduce.12.cloned.1.call-update
  531.1 0.0 all-reduce.14.cloned.1.call-start
  531.2 68.7 %all-reduce.12.cloned.1.call-done = f32[32,1024]{1,0:T(8,128)} async-done(((f32[32,1024]{1,0:T(8,128)}), f32[32,1024]{1,0:T(8,128)}) %all-reduce.12.cloned.1.call-update) | async-done | bytes 131088 | tf_op jit(solution)/shard_map/psum | solution.py:33
  599.9 0.9 add_log_fusion
  600.9 7.2 all_gather.7
  608.0 0.9 copy-done.6
  608.9 1.0 log_add_fusion
  609.9 1.6 copy.47
  611.6 27.7 %gather_fusion.1 = f32[8192,32]{1,0:T(8,128)} fusion(f32[32,4096]{0,1:T(8,128)S(1)} %copy.47, s32[8192]{0:T(1024)S(1)} %fusion.12), kind=kCustom, calls=%fused_computation.1.clone | custom fusion | bytes 2129920 | tf_op jit(solution)/shard_map/jit(_take)/gather | solution.py:36
  639.3 6.5 fusion.9
  645.8 0.0 copy-done.1
  645.8 0.0 copy-done.3
  645.9 4.0 exponential_reduce_fusion
  649.9 0.2 subtract_reduce_fusion
  650.1 39.0 %pmax.15 = f32[32]{0:T(128)S(1)} all-reduce(f32[32]{0:T(128)S(1)} %subtract_reduce_fusion), channel_id=1, replica_groups=mesh['traj'=8,'mstate'=4] {'traj','mstate'}, use_global_device_ids=true, to_apply=%region_15.17 | all-reduce | flops 32 | bytes 256 | tf_op jit(solution)/shard_map/pmax | solution.py:40
  689.1 0.2 exponential_bitcast_fusion
  689.3 2.6 copy.49
  691.9 45.7 %scatter_custom_fusion.2 = f32[4096,32]{1,0:T(8,128)} fusion(s32[8192]{0:T(1024)S(1)} %copy-done.10, f32[8192,32]{1,0:T(8,128)} %copy.49, f32[]{:T(128)} %constant.11.clone.1), kind=kCustom, calls=%fused_computation.17 | custom fusion | flops 262144 | bytes 524800 | tf_op jit(solution)/shard_map/scatter-add | solution.py:42
  737.7 0.0 all-reduce.14.cloned.1.call-update
  737.7 1.6 constant_dynamic-slice_fusion
  739.3 132.6 %all-reduce.14.cloned.1.call-done = f32[32,4096]{0,1:T(8,128)} async-done(((f32[32,4096]{0,1:T(8,128)}), f32[32,4096]{0,1:T(8,128)}) %all-reduce.14.cloned.1.call-update) | async-done | bytes 524304 | tf_op jit(solution)/shard_map/psum | solution.py:43
  871.9 1.1 fusion.11
  873.0 0.8 copy.50
  (19 shorter events, 0.1 us)
Async XLA Ops:
  7.2 102.7 %all-reduce.6.cloned.1.call-start = ((), (), s32[]{:S(2)}) async-start(), calls=%async_computation | async-start | bytes 262144 | tf_op jit(solution)/shard_map/psum | solution.py:33
  9.1 28.4 %copy-start.10 = (s32[8192]{0:T(1024)S(1)}, s32[8192]{0:T(1024)}, u32[]{:S(2)}) copy-start(s32[8192]{0:T(1024)} %param.9) | copy-start | bytes 98308
  9.1 28.4 %copy-start.11 = (s32[8192]{0:T(1024)S(1)}, s32[8192]{0:T(1024)}, u32[]{:S(2)}) copy-start(s32[8192]{0:T(1024)} %param.10) | copy-start | bytes 98308
  37.4 50.2 %copy-start.2 = (f32[32,8192]{1,0:T(8,128)S(1)}, f32[32,8192]{1,0:T(8,128)}, u32[]{:S(2)}) copy-start(f32[32,8192]{1,0:T(8,128)} %param.8) | copy-start | bytes 3145732
  37.4 205.7 %all-reduce.8.cloned.1.call-start = ((), (), s32[]{:S(2)}) async-start(), calls=%async_computation.1 | async-start | bytes 1048576 | tf_op jit(solution)/shard_map/psum | solution.py:18
  87.5 155.7 %copy-start.9 = (f32[32,4096]{1,0:T(8,128)S(1)}, f32[32,4096]{1,0:T(8,128)}, u32[]{:S(2)}) copy-start(f32[32,4096]{1,0:T(8,128)} %param.12) | copy-start | bytes 1572868
  87.5 414.0 %all-reduce.10.cloned.1.call-start = ((), (), s32[]{:S(2)}) async-start(), calls=%async_computation.2 | async-start | bytes 1048576 | tf_op jit(solution)/shard_map/psum | solution.py:43
  118.0 125.2 %copy-start.5 = (f32[32,4096]{1,0:T(8,128)}, f32[32,4096]{1,0:T(8,128)S(1)}, u32[]{:S(2)}) copy-start(f32[32,4096]{1,0:T(8,128)S(1)} %all_gather.6) | copy-start | bytes 1572868
  274.5 6.5 copy-start
  274.5 6.5 copy-start.4
  373.7 226.2 %all-reduce.12.cloned.1.call-start = ((), (), s32[]{:S(2)}) async-start(), calls=%async_computation.3 | async-start | bytes 262144 | tf_op jit(solution)/shard_map/psum | solution.py:33
  502.8 106.1 %copy-start.7 = (f32[32,4096]{1,0:T(8,128)S(1)}, f32[32,4096]{1,0:T(8,128)}, u32[]{:S(2)}) copy-start(f32[32,4096]{1,0:T(8,128)} %all-reduce.10.cloned.1.call-done) | copy-start | bytes 1572868
  502.8 106.1 %copy-start.8 = (f32[32,4096]{1,0:T(8,128)S(1)}, f32[32,4096]{1,0:T(8,128)}, u32[]{:S(2)}) copy-start(f32[32,4096]{1,0:T(8,128)} %all-reduce.8.cloned.1.call-done) | copy-start | bytes 1572868
  531.1 340.8 %all-reduce.14.cloned.1.call-start = ((), (), s32[]{:S(2)}) async-start(), calls=%async_computation.4 | async-start | bytes 4194304 | tf_op jit(solution)/shard_map/psum | solution.py:43
  608.0 0.9 copy-start.6
  639.3 6.5 copy-start.1
  639.3 6.5 copy-start.3
Sparse Core Ops, SparseCore 0:
  37.5 72.3 all-reduce.5
  116.0 127.0 all-reduce.7
  373.8 127.6 all-reduce.9
  531.3 68.6 all-reduce.11
  737.8 134.0 all-reduce.13
where the time goes:
time: 881 us; the launch traced here: 880 us
  waiting for transfers between devices  472 us (54%)
  other arithmetic  225 us (26%)
  blocking collectives  92.5 us (10%)
  local copies, waits for them, and re-layouts  76.5 us (9%)
  between operations  14 us (2%)
    psum x2, waiting for transfers between devices, per_device(): total = lax.psum(local_total, ('traj', 'mstate'))  259 us
    psum x1, waiting for transfers between devices, per_device(): visits = lax.psum(local_visits, ('traj', 'mstate'))  125 us
    scatter-add x2, other arithmetic, per_device(): local_total = jax.ops.segment_sum(weights.T, labels, num_segments=width).T  90.5 us
    psum x2, waiting for transfers between devices, per_device(): row_total = lax.psum(partial_rows, 'traj')  88.4 us
    pmax x2, blocking collectives, per_device(): shift = lax.pmax(jnp.max(term, axis=1), ('traj', 'mstate'))  78.2 us
    reduce_sum x2, other arithmetic, per_device(): partial_rows = jnp.sum(counts_real * weight, axis=1)  56.6 us
    gather x2, local copies, waits for them, and re-layouts, per_device(): scores = jnp.take(level, labels, axis=1) - bias  55.5 us
    scatter-add x1, other arithmetic, per_device(): local_visits = jax.ops.segment_sum(states, labels, num_segments=width).T  48.6 us
  transfers between devices with their start and end apart: 5, of which 5 were waited for; matrix products, arithmetic and copies ran while one was open for 6% of the time, Pallas kernels for 0%

commit v1 on v0

v1 whole, which is shorter than its diff:
```python
import functools

import jax
import jax.numpy as jnp
from jax import lax
from jax.experimental import pallas as pl
from jax.experimental.pallas import tpu as pltpu
from jax.sharding import PartitionSpec as P

ITERS = 2
LANES = 128
MESH = pl.DeviceIdType.MESH
VMEM = pl.BlockSpec(memory_space=pltpu.VMEM)
LIMIT = 48 * 1024 * 1024


def mult_kernel(where, counts, rows, cols, out, spread):
    k = pl.program_id(0)
    chunks = rows.shape[0]
    for piece in range(cols.shape[0]):
        line = cols[piece, pl.ds(k, 1), :]
        spread[pl.ds(piece * LANES, LANES), :] = jnp.transpose(
            jnp.broadcast_to(line, (LANES, LANES))
        )
    own = [jnp.broadcast_to(rows[c, pl.ds(k, 1), :], (8, LANES)) for c in range(chunks)]

    def body(step, sums):
        at = pl.ds(pl.multiple_of(step * 8, 8), 8)
        other = spread[at, :]
        made = []
        for c in range(chunks):
            number = counts[0, at, c * LANES : (c + 1) * LANES].astype(jnp.float32)
            made.append(sums[c] + number * (1.0 + jnp.tanh(own[c] - other)))
        return tuple(made)

    zero = jnp.zeros((8, LANES), jnp.float32)
    sums = lax.fori_loop(0, counts.shape[1] // 8, body, (zero,) * chunks, unroll=4)
    for c in range(chunks):
        out[c, pl.ds(k, 1), :] = 0.5 * jnp.sum(sums[c], axis=0, keepdims=True)


def mult_partial(where, counts, half):
    states_k, cols, rows = counts.shape
    r, c = rows // LANES, cols // LANES
    return pl.pallas_call(
        mult_kernel,
        grid_spec=pltpu.PrefetchScalarGridSpec(
            num_scalar_prefetch=1,
            grid=(states_k,),
            in_specs=[
                pl.BlockSpec((1, cols, rows), lambda k, w: (k, 0, 0)),
                pl.BlockSpec((r, states_k, LANES), lambda k, w: (w[1], 0, 0)),
                pl.BlockSpec((c, states_k, LANES), lambda k, w: (w[0], 0, 0)),
            ],
            out_specs=pl.BlockSpec((r, states_k, LANES), lambda k, w: (0, 0, 0)),
            scratch_shapes=[pltpu.VMEM((cols, LANES), jnp.float32)],
        ),
        out_shape=jax.ShapeDtypeStruct((r, states_k, LANES), jnp.float32),
        compiler_params=pltpu.CompilerParams(vmem_limit_bytes=LIMIT),
        name="mult_partial",
    )(where, counts, half, half)


def low_onehot(lab):
    low = jnp.bitwise_and(lab, 255)
    lines = lax.broadcasted_iota(jnp.int32, (256, lab.shape[1]), 0)
    return jnp.where(lines == low, 1.0, 0.0).astype(jnp.bfloat16)


def dot_nt(a, b):
    return lax.dot_general(
        a, b, (((1,), (1,)), ((), ())), preferred_element_type=jnp.float32
    )


def visits_kernel(tile, states_k, labels, therm, out, left, acc):
    highs = out.shape[0] // 2
    acc[...] = jnp.zeros_like(acc)

    @pl.loop(0, labels.shape[1] // tile)
    def _(step):
        at = pl.ds(pl.multiple_of(step * tile, tile), tile)
        lab = labels[:, at]
        high = jnp.right_shift(lab, 8)
        lines = lax.broadcasted_iota(jnp.int32, (states_k, tile), 0)
        member = jnp.where(lines == therm[:, at], 1.0, 0.0)
        for h in range(highs):
            left[pl.ds(h * states_k, states_k), :] = jnp.where(
                high == h, member, 0.0
            ).astype(jnp.bfloat16)
        acc[...] += dot_nt(left[...], low_onehot(lab))

    for h in range(highs):
        at = pl.ds(h * states_k, states_k)
        out[2 * h] = acc[at, :LANES]
        out[2 * h + 1] = acc[at, LANES:]


def local_visits(labels, therm, states_k, width):
    tile = 1024
    rows = width // 256 * states_k
    return pl.pallas_call(
        functools.partial(visits_kernel, tile, states_k),
        out_shape=jax.ShapeDtypeStruct((width // LANES, states_k, LANES), jnp.float32),
        in_specs=[VMEM] * 2,
        out_specs=VMEM,
        scratch_shapes=[
            pltpu.VMEM((rows, tile), jnp.bfloat16),
            pltpu.VMEM((rows, 256), jnp.float32),
        ],
        compiler_params=pltpu.CompilerParams(vmem_limit_bytes=LIMIT),
        name="local_visits",
    )(labels, therm)


def frames_kernel(tile, bias, labels, table, out, term, left, acc):
    chunks, states_k, _ = table.shape
    frames = bias.shape[1]
    groups = states_k // 8

    def pick(step, top_term):
        at = pl.ds(pl.multiple_of(step * LANES, LANES), LANES)
        lab = jnp.broadcast_to(labels[:, at], (8, LANES))
        low = jnp.bitwise_and(lab, LANES - 1)
        high = jnp.right_shift(lab, 7)
        found = [jnp.zeros((8, LANES), jnp.float32)] * groups
        for c in range(chunks):
            here = high == c
            for g in range(groups):
                piece = table[c, g * 8 : (g + 1) * 8, :]
                value = jnp.take_along_axis(piece, low, axis=1)
                found[g] = jnp.where(here, value, found[g])
        cost = [bias[g * 8 : (g + 1) * 8, at] for g in range(groups)]
        scores = [found[g] - cost[g] for g in range(groups)]
        top = jnp.max(functools.reduce(jnp.maximum, scores), axis=0, keepdims=True)
        total = sum(jnp.exp(s - top) for s in scores)
        logl = top + jnp.log(jnp.sum(total, axis=0, keepdims=True))
        made = []
        for g in range(groups):
            value = -cost[g] - logl
            term[g * 8 : (g + 1) * 8, at] = value
            made.append(jnp.maximum(top_term[g], value))
        return tuple(made)

    start = (jnp.full((8, LANES), -jnp.inf, jnp.float32),) * groups
    best = lax.fori_loop(0, frames // LANES, pick, start)
    shift = jnp.concatenate([jnp.max(b, axis=1, keepdims=True) for b in best], axis=0)
    acc[...] = jnp.zeros_like(acc)
    highs = chunks // 2

    @pl.loop(0, frames // tile)
    def _(step):
        at = pl.ds(pl.multiple_of(step * tile, tile), tile)
        lab = labels[:, at]
        high = jnp.right_shift(lab, 8)
        weight = jnp.exp(term[:, at] - shift)
        coarse = weight.astype(jnp.bfloat16).astype(jnp.float32)
        fine = weight - coarse
        for h in range(highs):
            here = high == h
            left[pl.ds(h * states_k, states_k), :] = jnp.where(
                here, coarse, 0.0
            ).astype(jnp.bfloat16)
            left[pl.ds((highs + h) * states_k, states_k), :] = jnp.where(
                here, fine, 0.0
            ).astype(jnp.bfloat16)
        acc[...] += dot_nt(left[...], low_onehot(lab))

    for h in range(highs):
        total = acc[pl.ds(h * states_k, states_k), :] + acc[
            pl.ds((highs + h) * states_k, states_k), :
        ]
        logged = shift + jnp.log(total)
        out[2 * h] = logged[:, :LANES]
        out[2 * h + 1] = logged[:, LANES:]


def frame_sums(bias, labels, table):
    tile = 1024
    chunks, states_k, _ = table.shape
    rows = chunks * states_k
    return pl.pallas_call(
        functools.partial(frames_kernel, tile),
        out_shape=jax.ShapeDtypeStruct(table.shape, jnp.float32),
        in_specs=[VMEM] * 3,
        out_specs=VMEM,
        scratch_shapes=[
            pltpu.VMEM(bias.shape, jnp.float32),
            pltpu.VMEM((rows, tile), jnp.bfloat16),
            pltpu.VMEM((rows, 256), jnp.float32),
        ],
        compiler_params=pltpu.CompilerParams(vmem_limit_bytes=LIMIT),
        name="frame_sums",
    )(bias, labels, table)


class Place:
    def __init__(self, traj, mstate):
        self.traj, self.mstate, self.all = traj, mstate, traj * mstate
        self.t, self.m = lax.axis_index("traj"), lax.axis_index("mstate")
        self.p = self.t * mstate + self.m
        self.chunk = self.m * traj + self.t

    def other(self, o):
        q = lax.rem(self.p + o, self.all)
        t, m = lax.div(q, self.mstate), lax.rem(q, self.mstate)
        return q, t, m, m * self.traj + t

    def greet(self):
        barrier = pltpu.get_barrier_semaphore()

        @pl.loop(1, self.all)
        def _(o):
            _, t, m, _ = self.other(o)
            pl.semaphore_signal(barrier, inc=1, device_id=(t, m), device_id_type=MESH)

        pl.semaphore_wait(barrier, self.all - 1)


def remote(src, dst, send, recv, to):
    return pltpu.make_async_remote_copy(
        src_ref=src, dst_ref=dst, send_sem=send, recv_sem=recv,
        device_id=to, device_id_type=MESH,
    )


class Scatter:
    def __init__(self, place, src, held, send, recv):
        self.args = (place, src, held, send, recv)

    def start(self):
        place, src, held, send, recv = self.args

        @pl.loop(1, place.all)
        def _(o):
            _, t, m, c = place.other(o)
            remote(src.at[c], held.at[place.p], send.at[o], recv.at[o], (t, m)).start()

        held[place.p] = src[place.chunk]

    def wait(self):
        place, src, held, send, recv = self.args

        @pl.loop(1, place.all)
        def _(o):
            q, t, m, c = place.other(place.all - o)
            remote(src.at[c], held.at[q], send.at[o], recv.at[o], (t, m)).wait()


class Rows:
    def __init__(self, place, src, held, send, recv, each):
        self.args = (place, src, held, send, recv, each)

    def start(self):
        place, src, held, send, recv, each = self.args

        @pl.loop(1, place.traj)
        def _(o):
            t = lax.rem(place.t + o, place.traj)
            block = src.at[t] if each else src.at[place.t]
            remote(block, held.at[place.t], send.at[o], recv.at[o], (t, place.m)).start()

        if each:
            held[place.t] = src[place.t]

    def wait(self):
        place, src, held, send, recv, each = self.args

        @pl.loop(1, place.traj)
        def _(o):
            t = lax.rem(place.t + place.traj - o, place.traj)
            remote(src.at[t], held.at[t], send.at[o], recv.at[o], (t, place.m)).wait()


class Gather:
    def __init__(self, place, whole, send, recv):
        self.args = (place, whole, send, recv)

    def start(self):
        place, whole, send, recv = self.args

        @pl.loop(1, place.all)
        def _(o):
            _, t, m, _ = place.other(o)
            own = whole.at[place.chunk]
            remote(own, own, send.at[o], recv.at[o], (t, m)).start()

    def wait(self):
        place, whole, send, recv = self.args

        @pl.loop(1, place.all)
        def _(o):
            _, t, m, c = place.other(place.all - o)
            got = whole.at[c]
            remote(got, got, send.at[o], recv.at[o], (t, m)).wait()


def level_kernel(sizes, first, part, vis, free, level, mult, *rest):
    place = Place(*sizes)
    if first:
        vis_out, held, s0, r0, s1, r1, held_vis, s2, r2 = rest
    else:
        held, s0, r0, s1, r1 = rest
    place.greet()
    rows = Rows(place, part, held, s0, r0, True)
    rows.start()
    if first:
        scatter = Scatter(place, vis, held_vis, s2, r2)
        scatter.start()
    rows.wait()
    inner = 0.5 + sum(held[i] for i in range(place.traj))
    mult[...] = jnp.log(inner)
    if first:
        scatter.wait()
        visits = sum(held_vis[i] for i in range(place.all))
        vis_out[...] = visits
    else:
        visits = vis[...]
    level[place.chunk] = jnp.log(inner + visits) + free[...]
    gather = Gather(place, level, s1, r1)
    gather.start()
    gather.wait()


def levels(sizes, first, part, vis, free):
    traj, mstate = sizes
    every = traj * mstate
    block = part.shape[1:]
    one = jax.ShapeDtypeStruct(block, jnp.float32)
    dma = pltpu.SemaphoreType.DMA
    scratch = [pltpu.VMEM((traj, *block), jnp.float32), dma((traj,)), dma((traj,)), dma((every,)), dma((every,))]
    if first:
        scratch += [pltpu.VMEM((every, *block), jnp.float32), dma((every,)), dma((every,))]
    shapes = [jax.ShapeDtypeStruct((every, *block), jnp.float32), one] + [one] * first
    return pl.pallas_call(
        functools.partial(level_kernel, sizes, first),
        out_shape=shapes,
        in_specs=[VMEM] * 3,
        out_specs=[VMEM] * len(shapes),
        scratch_shapes=scratch,
        compiler_params=pltpu.CompilerParams(
            collective_id=0 if first else 1, has_side_effects=True, vmem_limit_bytes=LIMIT
        ),
        name="levels_first" if first else "levels_later",
    )(part, vis, free)


def free_kernel(sizes, last, logged, mult, out, *rest):
    place = Place(*sizes)
    if last:
        held, s0, r0, s1, r1 = rest
    else:
        free_out, held, s0, r0, s1, r1 = rest
    place.greet()
    scatter = Scatter(place, logged, held, s0, r0)
    scatter.start()
    scatter.wait()
    top = functools.reduce(jnp.maximum, [held[i] for i in range(place.all)])
    top = jnp.maximum(top, -3e38)
    total = sum(jnp.exp(held[i] - top) for i in range(place.all))
    free = -(top + jnp.log(total))
    if last:
        out[place.t, 0] = free
        out[place.t, 1] = mult[...]
        gather = Rows(place, out, out, s1, r1, False)
    else:
        free_out[...] = free
        out[place.chunk] = 0.5 * (mult[...] - free)
        gather = Gather(place, out, s1, r1)
    gather.start()
    gather.wait()


def free_energies(sizes, last, logged, mult):
    traj, mstate = sizes
    every = traj * mstate
    block = mult.shape
    dma = pltpu.SemaphoreType.DMA
    if last:
        shapes = [jax.ShapeDtypeStruct((traj, 2, *block), jnp.float32)]
        second = traj
    else:
        shapes = [jax.ShapeDtypeStruct(s, jnp.float32) for s in ((every, *block), block)]
        second = every
    return pl.pallas_call(
        functools.partial(free_kernel, sizes, last),
        out_shape=shapes,
        in_specs=[VMEM] * 2,
        out_specs=[VMEM] * len(shapes),
        scratch_shapes=[
            pltpu.VMEM((every, *block), jnp.float32),
            dma((every,)), dma((every,)), dma((second,)), dma((second,)),
        ],
        compiler_params=pltpu.CompilerParams(
            collective_id=3 if last else 2, has_side_effects=True, vmem_limit_bytes=LIMIT
        ),
        name="free_last" if last else "free_earlier",
    )(logged, mult)


def chunked(sizes, bias, labels, therm_index, counts, free_start, mult_start):
    states_k, width = free_start.shape
    every = sizes[0] * sizes[1]
    t, m = lax.axis_index("traj"), lax.axis_index("mstate")
    where = jnp.stack([t, m]).astype(jnp.int32)
    lab, therm = labels[None, :], therm_index[None, :]
    half = 0.5 * (mult_start - free_start)
    half = half.reshape(states_k, every, LANES).transpose(1, 0, 2)
    free = lax.dynamic_slice_in_dim(free_start, (m * sizes[0] + t) * LANES, LANES, 1)
    vis = local_visits(lab, therm, states_k, width)
    for step in range(ITERS):
        part = mult_partial(where, counts, half)
        if step == 0:
            table, mult, vis = levels(sizes, True, part, vis, free)
        else:
            table, mult = levels(sizes, False, part, vis, free)
        logged = frame_sums(bias, lab, table)
        if step < ITERS - 1:
            half, free = free_energies(sizes, False, logged, mult)
    (both,) = free_energies(sizes, True, logged, mult)
    both = both.transpose(1, 2, 0, 3).reshape(2, states_k, sizes[0] * LANES)
    return both[0], both[1]


def unchunked(bias, labels, therm_index, counts, free_start, mult_start):
    states_k = bias.shape[0]
    width = free_start.shape[1]
    col_count = counts.shape[1]
    row_count = counts.shape[2]
    col_start = lax.axis_index("traj") * col_count
    row_start = lax.axis_index("mstate") * row_count
    states = jax.nn.one_hot(therm_index, states_k, dtype=jnp.float32)
    visits = lax.psum(
        jax.ops.segment_sum(states, labels, num_segments=width).T, ("traj", "mstate")
    )
    counts_real = counts.astype(jnp.float32)
    free, mult = (free_start, mult_start)
    for step in range(ITERS):
        half = mult - free
        cols = lax.dynamic_slice_in_dim(half, col_start, col_count, 1)
        rows = lax.dynamic_slice_in_dim(half, row_start, row_count, 1)
        weight = jax.nn.sigmoid(rows[:, None, :] - cols[:, :, None])
        row_total = lax.psum(jnp.sum(counts_real * weight, axis=1), "traj")
        mult = lax.all_gather(jnp.log(0.5 + row_total), "mstate", axis=1, tiled=True)
        level = jnp.log(jnp.exp(mult) + visits) + free
        scores = jnp.take(level, labels, axis=1) - bias
        top = jnp.max(scores, axis=0)
        logl = top + jnp.log(jnp.sum(jnp.exp(scores - top[None, :]), axis=0))
        term = -bias - logl[None, :]
        shift = lax.pmax(jnp.max(term, axis=1), ("traj", "mstate"))
        weights = jnp.exp(term - shift[:, None])
        local_total = jax.ops.segment_sum(weights.T, labels, num_segments=width).T
        total = lax.psum(local_total, ("traj", "mstate"))
        free = -(shift[:, None] + jnp.log(total))
    free_out = lax.dynamic_slice_in_dim(free, row_start, row_count, 1)
    mult_out = lax.dynamic_slice_in_dim(mult, row_start, row_count, 1)
    return (free_out, mult_out)


def solution(mesh):
    sizes = (mesh.shape["traj"], mesh.shape["mstate"])

    def per_device(bias, labels, therm_index, counts, free_start, mult_start):
        args = (bias, labels, therm_index, counts, free_start, mult_start)
        fits = (
            free_start.shape[1] == sizes[0] * sizes[1] * LANES
            and counts.shape[1] % LANES == 0
            and bias.shape[1] % 1024 == 0
            and bias.shape[0] % 16 == 0
        )
        return chunked(sizes, *args) if fits else unchunked(*args)

    placed = (
        P(None, ("traj", "mstate")),
        P(("traj", "mstate")),
        P(("traj", "mstate")),
        P(None, "traj", "mstate"),
        P(),
        P(),
    )
    return jax.shard_map(
        per_device,
        mesh=mesh,
        in_specs=placed,
        out_specs=(P(None, "mstate"), P(None, "mstate")),
        check_vma=False,
    )
```

time: 881 us -> 250 us (0.28)
  waiting for transfers between devices: 472 us -> 0 us
  Pallas kernels: 0 us -> 242 us
  other arithmetic: 225 us -> 1.35 us
  blocking collectives: 92.5 us -> 0 us
  local copies, waits for them, and re-layouts: 76.5 us -> 3.24 us
  between operations: 14 us -> 0.76 us
    psum x5 -> x0, waiting for transfers between devices: 472 us -> none  [the longest x2 259 us: per_device(): total = lax.psum(local_total, ('traj', 'mstate'))]
    pallas_call x0 -> x9, Pallas kernels: none -> 242 us  [the longest x2 80.1 us: mult_partial(): pl.pallas_call(mult_kernel, grid_spec=pltpu.PrefetchScalarGridSpec(num_sc...]
    scatter-add x3 -> x0, other arithmetic: 139 us -> none  [the longest x2 90.5 us: per_device(): local_total = jax.ops.segment_sum(weights.T, labels, num_segments=width).T]
    pmax x2 -> x0, blocking collectives: 78.2 us -> none  [per_device(): shift = lax.pmax(jnp.max(term, axis=1), ('traj', 'mstate'))]
    reduce_sum x4 -> x0, other arithmetic: 64.6 us -> none  [the longest x2 56.6 us: per_device(): partial_rows = jnp.sum(counts_real * weight, axis=1)]
    gather x2 -> x0, local copies, waits for them, and re-layouts: 55.5 us -> none  [per_device(): scores = jnp.take(level, labels, axis=1) - bias]
    all_gather x2 -> x0, blocking collectives: 14.3 us -> none  [per_device(): lax.all_gather(jnp.log(0.5 + row_total), 'mstate', axis=1, tiled=True)]
    reduce_max x4 -> x0, other arithmetic: 13.5 us -> none  [the longest x2 13.1 us: per_device(): top = jnp.max(scores, axis=0)]
  transfers between devices with their start and end apart: 5 -> 0, of which waited for: 5 -> 0; matrix products, arithmetic and copies ran while one was open for 6% -> 0% of each run, Pallas kernels for 0% -> 0%
where the time goes in v1:
time: 250 us; the launch traced here: 247 us
  Pallas kernels  242 us (97%)
  local copies, waits for them, and re-layouts  3.24 us (1%)
    pallas_call x2, Pallas kernels, mult_partial(): pl.pallas_call(mult_kernel, grid_spec=pltpu.PrefetchScalarGridSpec(num_sc...  80.1 us
    pallas_call x2, Pallas kernels, free_energies(): pl.pallas_call(functools.partial(free_kernel, sizes, last), out_shape=sha...  58 us
    pallas_call x2, Pallas kernels, levels(): pl.pallas_call(functools.partial(level_kernel, sizes, first), out_shape=s...  55.8 us
    pallas_call x2, Pallas kernels, frame_sums(): pl.pallas_call(functools.partial(frames_kernel, tile), out_shape=jax.Shap...  44.2 us

profile of v1, /device:TPU:0, one launch (start us, length us, event | category | flops | bytes accessed | tf_op | source)
XLA Modules:
  0.0 247.4 jit_solution(519701699698661868)
XLA Ops:
  0.6 0.0 copy-start
  0.6 0.1 pad_add_fusion.where
  0.7 0.8 constant_dynamic-slice_fusion.free
  1.5 0.0 copy-start.1
  1.5 0.8 copy-done.1
  2.3 0.0 copy-start.3
  2.3 0.8 copy-done.3
  3.0 0.0 copy-start.2
  3.0 3.9 %local_visits.1.vis = f32[32,32,128]{2,1,0:T(8,128)S(1)} custom-call(s32[1,8192]{1,0:T(1,128)S(1)} %bitcast.21, s32[1,8192]{1,0:T(1,128)S(1)} %bitcast.24), custom_call_target="tpu_custom_call" | custom-call | tf_op jit(solution)/shard_map/local_visits/pallas_call | solution.py:102
  7.0 1.3 bitcast_bitcast_fusion.rows.cols
  8.3 40.1 %mult_partial.2.part = f32[8,32,128]{2,1,0:T(8,128)S(1)} custom-call(s32[2]{0:T(128)S(1)} %pad_add_fusion.where, s32[32,512,1024]{2,1,0:T(8,128)} %counts.3, f32[32,32,128]{2,1,0:T(8,128)S(1)} %bitcast_bitcast_fusion.rows.cols, f32[32,32,128]{2,1,0:T(8,128)S(1)} %bitcast_bitcast_fusion.rows.cols), custom_call_target="tpu_custom_call" | custom-call | tf_op jit(solution)/shard_map/mult_partial/pallas_call | solution.py:45
  48.3 30.2 %levels_first.1 = (f32[32,32,128]{2,1,0:T(8,128)S(1)}, f32[32,128]{1,0:T(8,128)S(1)}, f32[32,128]{1,0:T(8,128)S(1)}) custom-call(f32[8,32,128]{2,1,0:T(8,128)S(1)} %mult_partial.2.part, f32[32,32,128]{2,1,0:T(8,128)S(1)} %local_visits.1.vis, f32[32,128]{1,0:T(8,128)S(1)} %constant_dynamic-slice_fusion.free), custom_call_target="tpu_custom_call" | custom-call | tf_op jit(solution)/shard_map/levels_first/pallas_call | solution.py:335
  78.5 0.0 copy-done
  78.5 0.0 copy-done.2
  78.5 22.1 %frame_sums.2.logged = f32[32,32,128]{2,1,0:T(8,128)S(1)} custom-call(f32[32,8192]{1,0:T(8,128)S(1)} %copy-done, s32[1,8192]{1,0:T(1,128)S(1)} %bitcast.22, f32[32,32,128]{2,1,0:T(8,128)S(1)} %get-tuple-element.9.table), custom_call_target="tpu_custom_call" | custom-call | tf_op jit(solution)/shard_map/frame_sums/pallas_call | solution.py:182
  100.7 31.5 %free_earlier.1 = (f32[32,32,128]{2,1,0:T(8,128)S(1)}, f32[32,128]{1,0:T(8,128)S(1)}) custom-call(f32[32,32,128]{2,1,0:T(8,128)S(1)} %frame_sums.2.logged, f32[32,128]{1,0:T(8,128)S(1)} %get-tuple-element.10.mult), custom_call_target="tpu_custom_call" | custom-call | tf_op jit(solution)/shard_map/free_earlier/pallas_call | solution.py:385
  132.2 40.1 %mult_partial.3.part = f32[8,32,128]{2,1,0:T(8,128)S(1)} custom-call(s32[2]{0:T(128)S(1)} %pad_add_fusion.where, s32[32,512,1024]{2,1,0:T(8,128)} %counts.3, f32[32,32,128]{2,1,0:T(8,128)S(1)} %get-tuple-element.11.rows.cols, f32[32,32,128]{2,1,0:T(8,128)S(1)} %get-tuple-element.11.rows.cols), custom_call_target="tpu_custom_call" | custom-call | tf_op jit(solution)/shard_map/mult_partial/pallas_call | solution.py:45
  172.2 25.6 %levels_later.1 = (f32[32,32,128]{2,1,0:T(8,128)S(1)}, f32[32,128]{1,0:T(8,128)S(1)}) custom-call(f32[8,32,128]{2,1,0:T(8,128)S(1)} %mult_partial.3.part, f32[32,128]{1,0:T(8,128)S(1)} %get-tuple-element.12.vis, f32[32,128]{1,0:T(8,128)S(1)} %get-tuple-element.13.free), custom_call_target="tpu_custom_call" | custom-call | tf_op jit(solution)/shard_map/levels_later/pallas_call | solution.py:335
  197.8 22.1 %frame_sums.3.logged = f32[32,32,128]{2,1,0:T(8,128)S(1)} custom-call(f32[32,8192]{1,0:T(8,128)S(1)} %copy-done, s32[1,8192]{1,0:T(1,128)S(1)} %bitcast.23, f32[32,32,128]{2,1,0:T(8,128)S(1)} %get-tuple-element.14.table), custom_call_target="tpu_custom_call" | custom-call | tf_op jit(solution)/shard_map/frame_sums/pallas_call | solution.py:182
  219.9 26.5 %free_last.1 = f32[8,2,32,128]{3,2,1,0:T(8,128)S(1)} custom-call(f32[32,32,128]{2,1,0:T(8,128)S(1)} %frame_sums.3.logged, f32[32,128]{1,0:T(8,128)S(1)} %get-tuple-element.15.mult), custom_call_target="tpu_custom_call" | custom-call | tf_op jit(solution)/shard_map/free_last/pallas_call | solution.py:385
  246.5 0.1 copy.10
  246.6 0.1 copy.9
  246.6 0.7 copy_bitcast_fusion
  (1 shorter events, 0.0 us)
Async XLA Ops:
  0.6 77.9 %copy-start = (f32[32,8192]{1,0:T(8,128)S(1)}, f32[32,8192]{1,0:T(8,128)}, u32[]{:S(2)}) copy-start(f32[32,8192]{1,0:T(8,128)} %bias.3) | copy-start | bytes 3145732
  1.5 0.8 copy-start.1
  2.3 0.8 copy-start.3
  3.0 75.5 %copy-start.2 = (s32[8192]{0:T(1024)S(1)}, s32[8192]{0:T(1024)}, u32[]{:S(2)}) copy-start(s32[8192]{0:T(1024)} %param.7) | copy-start | bytes 98308

commit v2 on v1

--- a/solution.py
+++ b/solution.py
@@ -30,13 +30,15 @@
         made = []
         for c in range(chunks):
             number = counts[0, at, c * LANES : (c + 1) * LANES].astype(jnp.float32)
-            made.append(sums[c] + number * (1.0 + jnp.tanh(own[c] - other)))
+            whole = 1.0 + jnp.exp(jnp.minimum(other - own[c], 87.0))
+            near = pl.reciprocal(whole, approx=True)
+            made.append(sums[c] + (number * near) * (2.0 - whole * near))
         return tuple(made)
 
     zero = jnp.zeros((8, LANES), jnp.float32)
     sums = lax.fori_loop(0, counts.shape[1] // 8, body, (zero,) * chunks, unroll=4)
     for c in range(chunks):
-        out[c, pl.ds(k, 1), :] = 0.5 * jnp.sum(sums[c], axis=0, keepdims=True)
+        out[c, pl.ds(k, 1), :] = jnp.sum(sums[c], axis=0, keepdims=True)
 
 
 def mult_partial(where, counts, half):
@@ -196,25 +198,38 @@
 
 class Place:
     def __init__(self, traj, mstate):
-        self.traj, self.mstate, self.all = traj, mstate, traj * mstate
+        self.traj, self.mstate = traj, mstate
+        self.rows = 2 if traj % 2 == 0 else 1
+        self.planes = traj // self.rows
+        self.flat = self.rows * mstate
         self.t, self.m = lax.axis_index("traj"), lax.axis_index("mstate")
-        self.p = self.t * mstate + self.m
-        self.chunk = self.m * traj + self.t
-
-    def other(self, o):
-        q = lax.rem(self.p + o, self.all)
-        t, m = lax.div(q, self.mstate), lax.rem(q, self.mstate)
-        return q, t, m, m * self.traj + t
+        self.z, self.y = lax.div(self.t, self.rows), lax.rem(self.t, self.rows)
+        self.g = self.y * mstate + self.m
+
+    def beside(self, o):
+        q = lax.rem(self.g + o, self.flat)
+        return q, lax.div(q, self.mstate), lax.rem(q, self.mstate)
+
+    def plane(self, o):
+        return lax.rem(self.z + o, self.planes)
+
+    def at(self, z, y, m):
+        return (z * self.rows + y, m)
 
     def greet(self):
         barrier = pltpu.get_barrier_semaphore()
-
-        @pl.loop(1, self.all)
-        def _(o):
-            _, t, m, _ = self.other(o)
-            pl.semaphore_signal(barrier, inc=1, device_id=(t, m), device_id_type=MESH)
-
-        pl.semaphore_wait(barrier, self.all - 1)
+        for o in range(1, self.flat):
+            _, y, m = self.beside(o)
+            pl.semaphore_signal(
+                barrier, inc=1, device_id=self.at(self.z, y, m), device_id_type=MESH
+            )
+        for o in range(1, self.planes):
+            for y in range(self.rows):
+                pl.semaphore_signal(
+                    barrier, inc=1, device_id=self.at(self.plane(o), y, self.m),
+                    device_id_type=MESH,
+                )
+        pl.semaphore_wait(barrier, self.flat - 1 + (self.planes - 1) * self.rows)
 
 
 def remote(src, dst, send, recv, to):
@@ -224,27 +239,80 @@
     )
 
 
+def add_all(blocks):
+    return sum(blocks)
+
+
+def add_logs(blocks):
+    top = jnp.maximum(functools.reduce(jnp.maximum, blocks), -3e38)
+    return top + jnp.log(sum(jnp.exp(b - top) for b in blocks))
+
+
 class Scatter:
-    def __init__(self, place, src, held, send, recv):
-        self.args = (place, src, held, send, recv)
+    def __init__(self, place, join, src, near, stage, far, s0, r0, s1, r1):
+        self.place, self.join = place, join
+        self.src, self.near, self.stage, self.far = src, near, stage, far
+        self.s0, self.r0, self.s1, self.r1 = s0, r0, s1, r1
 
     def start(self):
-        place, src, held, send, recv = self.args
-
-        @pl.loop(1, place.all)
-        def _(o):
-            _, t, m, c = place.other(o)
-            remote(src.at[c], held.at[place.p], send.at[o], recv.at[o], (t, m)).start()
-
-        held[place.p] = src[place.chunk]
-
-    def wait(self):
-        place, src, held, send, recv = self.args
-
-        @pl.loop(1, place.all)
-        def _(o):
-            q, t, m, c = place.other(place.all - o)
-            remote(src.at[c], held.at[q], send.at[o], recv.at[o], (t, m)).wait()
+        p = self.place
+        for o in range(1, p.flat):
+            _, y, m = p.beside(o)
+            remote(
+                self.src.at[m, :, y], self.near.at[p.g], self.s0.at[o], self.r0.at[o],
+                p.at(p.z, y, m),
+            ).start()
+        for z in range(p.planes):
+            self.near[p.g, z] = self.src[p.m, z, p.y]
+
+    def middle(self):
+        p = self.place
+        for o in range(1, p.flat):
+            q, y, m = p.beside(p.flat - o)
+            remote(
+                self.src.at[m, :, y], self.near.at[q], self.s0.at[o], self.r0.at[o],
+                p.at(p.z, y, m),
+            ).wait()
+        for z in range(p.planes):
+            self.stage[z] = self.join([self.near[i, z] for i in range(p.flat)])
+        for o in range(1, p.planes):
+            z = p.plane(o)
+            remote(
+                self.stage.at[z], self.far.at[p.z], self.s1.at[o], self.r1.at[o],
+                p.at(z, p.y, p.m),
+            ).start()
+        self.far[p.z] = self.stage[p.z]
+
+    def finish(self):
+        p = self.place
+        for o in range(1, p.planes):
+            z = p.plane(p.planes - o)
+            remote(
+                self.stage.at[z], self.far.at[z], self.s1.at[o], self.r1.at[o],
+                p.at(z, p.y, p.m),
+            ).wait()
+        return self.join([self.far[i] for i in range(p.planes)])
+
+
+def scatter_scratch(sizes, block):
+    rows = 2 if sizes[0] % 2 == 0 else 1
+    planes, flat = sizes[0] // rows, rows * sizes[1]
+    dma = pltpu.SemaphoreType.DMA
+    return [
+        pltpu.VMEM((flat, planes, *block), jnp.float32),
+        pltpu.VMEM((planes, *block), jnp.float32),
+        pltpu.VMEM((planes, *block), jnp.float32),
+        dma((flat,)), dma((flat,)), dma((planes,)), dma((planes,)),
+    ]
+
+
+def gather_scratch(sizes):
+    return scatter_scratch(sizes, (8, LANES))[3:]
+
+
+def split_shape(sizes, block):
+    rows = 2 if sizes[0] % 2 == 0 else 1
+    return (sizes[1], sizes[0] // rows, rows, *block)
 
 
 class Rows:
@@ -272,67 +340,62 @@
             remote(src.at[t], held.at[t], send.at[o], recv.at[o], (t, place.m)).wait()
 
 
-class Gather:
-    def __init__(self, place, whole, send, recv):
-        self.args = (place, whole, send, recv)
-
-    def start(self):
-        place, whole, send, recv = self.args
-
-        @pl.loop(1, place.all)
-        def _(o):
-            _, t, m, _ = place.other(o)
-            own = whole.at[place.chunk]
-            remote(own, own, send.at[o], recv.at[o], (t, m)).start()
-
-    def wait(self):
-        place, whole, send, recv = self.args
-
-        @pl.loop(1, place.all)
-        def _(o):
-            _, t, m, c = place.other(place.all - o)
-            got = whole.at[c]
-            remote(got, got, send.at[o], recv.at[o], (t, m)).wait()
+def gather_all(p, whole, s0, r0, s1, r1):
+    own = whole.at[p.m, p.z, p.y]
+    for o in range(1, p.planes):
+        remote(own, own, s1.at[o], r1.at[o], p.at(p.plane(o), p.y, p.m)).start()
+    for o in range(1, p.planes):
+        z = p.plane(p.planes - o)
+        got = whole.at[p.m, z, p.y]
+        remote(got, got, s1.at[o], r1.at[o], p.at(z, p.y, p.m)).wait()
+    column = whole.at[p.m, :, p.y]
+    for o in range(1, p.flat):
+        _, y, m = p.beside(o)
+        remote(column, column, s0.at[o], r0.at[o], p.at(p.z, y, m)).start()
+    for o in range(1, p.flat):
+        _, y, m = p.beside(p.flat - o)
+        got = whole.at[m, :, y]
+        remote(got, got, s0.at[o], r0.at[o], p.at(p.z, y, m)).wait()
 
 
 def level_kernel(sizes, first, part, vis, free, level, mult, *rest):
     place = Place(*sizes)
     if first:
-        vis_out, held, s0, r0, s1, r1, held_vis, s2, r2 = rest
+        vis_out, held, s, r, *rest = rest
     else:
-        held, s0, r0, s1, r1 = rest
+        held, s, r, *rest = rest
     place.greet()
-    rows = Rows(place, part, held, s0, r0, True)
+    rows = Rows(place, part, held, s, r, True)
     rows.start()
     if first:
-        scatter = Scatter(place, vis, held_vis, s2, r2)
+        scatter = Scatter(place, add_all, vis, *rest[4:])
         scatter.start()
+        scatter.middle()
     rows.wait()
     inner = 0.5 + sum(held[i] for i in range(place.traj))
     mult[...] = jnp.log(inner)
     if first:
-        scatter.wait()
-        visits = sum(held_vis[i] for i in range(place.all))
+        visits = scatter.finish()
         vis_out[...] = visits
     else:
         visits = vis[...]
-    level[place.chunk] = jnp.log(inner + visits) + free[...]
-    gather = Gather(place, level, s1, r1)
-    gather.start()
-    gather.wait()
+    level[place.m, place.z, place.y] = jnp.log(inner + visits) + free[...]
+    gather_all(place, level, *rest[:4])
 
 
 def levels(sizes, first, part, vis, free):
-    traj, mstate = sizes
-    every = traj * mstate
+    traj = sizes[0]
     block = part.shape[1:]
     one = jax.ShapeDtypeStruct(block, jnp.float32)
     dma = pltpu.SemaphoreType.DMA
-    scratch = [pltpu.VMEM((traj, *block), jnp.float32), dma((traj,)), dma((traj,)), dma((every,)), dma((every,))]
+    scratch = [pltpu.VMEM((traj, *block), jnp.float32), dma((traj,)), dma((traj,))]
+    scratch += gather_scratch(sizes)
     if first:
-        scratch += [pltpu.VMEM((every, *block), jnp.float32), dma((every,)), dma((every,))]
-    shapes = [jax.ShapeDtypeStruct((every, *block), jnp.float32), one] + [one] * first
-    return pl.pallas_call(
+        scratch += scatter_scratch(sizes, block)
+        vis = vis.reshape(split_shape(sizes, block))
+    whole = jax.ShapeDtypeStruct(split_shape(sizes, block), jnp.float32)
+    shapes = [whole, one] + [one] * first
+    table, *others = pl.pallas_call(
         functools.partial(level_kernel, sizes, first),
         out_shape=shapes,
         in_specs=[VMEM] * 3,
@@ -343,59 +406,54 @@
         ),
         name="levels_first" if first else "levels_later",
     )(part, vis, free)
+    return table.reshape(-1, *block), *others
 
 
 def free_kernel(sizes, last, logged, mult, out, *rest):
     place = Place(*sizes)
-    if last:
-        held, s0, r0, s1, r1 = rest
-    else:
-        free_out, held, s0, r0, s1, r1 = rest
+    if not last:
+        free_out, *rest = rest
     place.greet()
-    scatter = Scatter(place, logged, held, s0, r0)
+    scatter = Scatter(place, add_logs, logged, *rest[:7])
     scatter.start()
-    scatter.wait()
-    top = functools.reduce(jnp.maximum, [held[i] for i in range(place.all)])
-    top = jnp.maximum(top, -3e38)
-    total = sum(jnp.exp(held[i] - top) for i in range(place.all))
-    free = -(top + jnp.log(total))
+    scatter.middle()
+    free = -scatter.finish()
     if last:
         out[place.t, 0] = free
         out[place.t, 1] = mult[...]
-        gather = Rows(place, out, out, s1, r1, False)
+        rows = Rows(place, out, out, *rest[7:], False)
+        rows.start()
+        rows.wait()
     else:
         free_out[...] = free
-        out[place.chunk] = 0.5 * (mult[...] - free)
-        gather = Gather(place, out, s1, r1)
-    gather.start()
-    gather.wait()
+        out[place.m, place.z, place.y] = mult[...] - free
+        gather_all(place, out, *rest[7:])
 
 
 def free_energies(sizes, last, logged, mult):
-    traj, mstate = sizes
-    every = traj * mstate
+    traj = sizes[0]
     block = mult.shape
+    split = split_shape(sizes, block)
     dma = pltpu.SemaphoreType.DMA
+    scratch = scatter_scratch(sizes, block)
     if last:
         shapes = [jax.ShapeDtypeStruct((traj, 2, *block), jnp.float32)]
-        second = traj
+        scratch += [dma((traj,)), dma((traj,))]
     else:
-        shapes = [jax.ShapeDtypeStruct(s, jnp.float32) for s in ((every, *block), block)]
-        second = every
-    return pl.pallas_call(
+        shapes = [jax.ShapeDtypeStruct(a, jnp.float32) for a in (split, block)]
+        scratch += gather_scratch(sizes)
+    made = pl.pallas_call(
         functools.partial(free_kernel, sizes, last),
         out_shape=shapes,
         in_specs=[VMEM] * 2,
         out_specs=[VMEM] * len(shapes),
-        scratch_shapes=[
-            pltpu.VMEM((every, *block), jnp.float32),
-            dma((every,)), dma((every,)), dma((second,)), dma((second,)),
-        ],
+        scratch_shapes=scratch,
         compiler_params=pltpu.CompilerParams(
             collective_id=3 if last else 2, has_side_effects=True, vmem_limit_bytes=LIMIT
         ),
         name="free_last" if last else "free_earlier",
-    )(logged, mult)
+    )(logged.reshape(split), mult)
+    return made if last else (made[0].reshape(-1, *block), made[1])
 
 
 def chunked(sizes, bias, labels, therm_index, counts, free_start, mult_start):
@@ -404,7 +462,7 @@
     t, m = lax.axis_index("traj"), lax.axis_index("mstate")
     where = jnp.stack([t, m]).astype(jnp.int32)
     lab, therm = labels[None, :], therm_index[None, :]
-    half = 0.5 * (mult_start - free_start)
+    half = mult_start - free_start
     half = half.reshape(states_k, every, LANES).transpose(1, 0, 2)
     free = lax.dynamic_slice_in_dim(free_start, (m * sizes[0] + t) * LANES, LANES, 1)
     vis = local_visits(lab, therm, states_k, width)

time: 250 us -> 241 us (0.964)
  Pallas kernels: 242 us -> 234 us
    pallas_call x2, Pallas kernels: 80.1 us -> 95.2 us  [mult_partial(): pl.pallas_call(mult_kernel, grid_spec=pltpu.PrefetchScalarGridSpec(num_sc...]
    pallas_call x2, Pallas kernels: 58 us -> 44.4 us  [free_energies(): pl.pallas_call(functools.partial(free_kernel, sizes, last), out_shape=sha...]
    pallas_call x2, Pallas kernels: 55.8 us -> 46.5 us  [levels(): pl.pallas_call(functools.partial(level_kernel, sizes, first), out_shape=s...]
where the time goes in v2:
time: 241 us; the launch traced here: 240 us
  Pallas kernels  234 us (97%)
  local copies, waits for them, and re-layouts  3.24 us (1%)
    pallas_call x2, Pallas kernels, mult_partial(): pl.pallas_call(mult_kernel, grid_spec=pltpu.PrefetchScalarGridSpec(num_sc...  95.2 us
    pallas_call x2, Pallas kernels, levels(): pl.pallas_call(functools.partial(level_kernel, sizes, first), out_shape=s...  46.5 us
    pallas_call x2, Pallas kernels, free_energies(): pl.pallas_call(functools.partial(free_kernel, sizes, last), out_shape=sha...  44.4 us
    pallas_call x2, Pallas kernels, frame_sums(): pl.pallas_call(functools.partial(frames_kernel, tile), out_shape=jax.Shap...  44.2 us

profile of v2, /device:TPU:0, one launch (start us, length us, event | category | flops | bytes accessed | tf_op | source)
XLA Modules:
  0.0 239.6 jit_solution(2929228653560852526)
XLA Ops:
  0.6 0.0 copy-start
  0.6 0.1 pad_add_fusion.where
  0.7 0.8 constant_dynamic-slice_fusion.free
  1.5 0.0 copy-start.1
  1.5 0.8 copy-done.1
  2.3 0.0 copy-start.3
  2.3 0.8 copy-done.3
  3.0 0.0 copy-start.2
  3.0 3.9 %local_visits.1 = f32[32,32,128]{2,1,0:T(8,128)S(1)} custom-call(s32[1,8192]{1,0:T(1,128)S(1)} %bitcast.34, s32[1,8192]{1,0:T(1,128)S(1)} %bitcast.37), custom_call_target="tpu_custom_call" | custom-call | tf_op jit(solution)/shard_map/local_visits/pallas_call | solution.py:104
  7.0 1.3 bitcast_bitcast_fusion.rows.cols
  8.2 47.6 %mult_partial.2.part = f32[8,32,128]{2,1,0:T(8,128)S(1)} custom-call(s32[2]{0:T(128)S(1)} %pad_add_fusion.where, s32[32,512,1024]{2,1,0:T(8,128)} %counts.3, f32[32,32,128]{2,1,0:T(8,128)S(1)} %bitcast_bitcast_fusion.rows.cols, f32[32,32,128]{2,1,0:T(8,128)S(1)} %bitcast_bitcast_fusion.rows.cols), custom_call_target="tpu_custom_call" | custom-call | tf_op jit(solution)/shard_map/mult_partial/pallas_call | solution.py:47
  55.9 28.4 %levels_first.1 = (f32[4,4,2,32,128]{4,3,2,1,0:T(8,128)S(1)}, f32[32,128]{1,0:T(8,128)S(1)}, f32[32,128]{1,0:T(8,128)S(1)}) custom-call(f32[8,32,128]{2,1,0:T(8,128)S(1)} %mult_partial.2.part, f32[4,4,2,32,128]{4,3,2,1,0:T(8,128)S(1)} %bitcast.28, f32[32,128]{1,0:T(8,128)S(1)} %constant_dynamic-slice_fusion.free), custom_call_target="tpu_custom_call" | custom-call | tf_op jit(solution)/shard_map/levels_first/pallas_call | solution.py:398
  84.3 0.0 copy-done
  84.3 0.0 copy-done.2
  84.3 22.1 %frame_sums.2 = f32[32,32,128]{2,1,0:T(8,128)S(1)} custom-call(f32[32,8192]{1,0:T(8,128)S(1)} %copy-done, s32[1,8192]{1,0:T(1,128)S(1)} %bitcast.35, f32[32,32,128]{2,1,0:T(8,128)S(1)} %bitcast.32), custom_call_target="tpu_custom_call" | custom-call | tf_op jit(solution)/shard_map/frame_sums/pallas_call | solution.py:184
  106.5 23.8 %free_earlier.1 = (f32[4,4,2,32,128]{4,3,2,1,0:T(8,128)S(1)}, f32[32,128]{1,0:T(8,128)S(1)}) custom-call(f32[4,4,2,32,128]{4,3,2,1,0:T(8,128)S(1)} %bitcast.29, f32[32,128]{1,0:T(8,128)S(1)} %get-tuple-element.10.mult), custom_call_target="tpu_custom_call" | custom-call | tf_op jit(solution)/shard_map/free_earlier/pallas_call | solution.py:445
  130.3 47.6 %mult_partial.3.part = f32[8,32,128]{2,1,0:T(8,128)S(1)} custom-call(s32[2]{0:T(128)S(1)} %pad_add_fusion.where, s32[32,512,1024]{2,1,0:T(8,128)} %counts.3, f32[32,32,128]{2,1,0:T(8,128)S(1)} %bitcast.26, f32[32,32,128]{2,1,0:T(8,128)S(1)} %bitcast.27), custom_call_target="tpu_custom_call" | custom-call | tf_op jit(solution)/shard_map/mult_partial/pallas_call | solution.py:47
  177.9 18.0 %levels_later.1 = (f32[4,4,2,32,128]{4,3,2,1,0:T(8,128)S(1)}, f32[32,128]{1,0:T(8,128)S(1)}) custom-call(f32[8,32,128]{2,1,0:T(8,128)S(1)} %mult_partial.3.part, f32[32,128]{1,0:T(8,128)S(1)} %get-tuple-element.12.vis, f32[32,128]{1,0:T(8,128)S(1)} %get-tuple-element.13.free), custom_call_target="tpu_custom_call" | custom-call | tf_op jit(solution)/shard_map/levels_later/pallas_call | solution.py:398
  196.0 22.1 %frame_sums.3 = f32[32,32,128]{2,1,0:T(8,128)S(1)} custom-call(f32[32,8192]{1,0:T(8,128)S(1)} %copy-done, s32[1,8192]{1,0:T(1,128)S(1)} %bitcast.36, f32[32,32,128]{2,1,0:T(8,128)S(1)} %bitcast.33), custom_call_target="tpu_custom_call" | custom-call | tf_op jit(solution)/shard_map/frame_sums/pallas_call | solution.py:184
  218.1 20.6 %free_last.1 = f32[8,2,32,128]{3,2,1,0:T(8,128)S(1)} custom-call(f32[4,4,2,32,128]{4,3,2,1,0:T(8,128)S(1)} %bitcast.30, f32[32,128]{1,0:T(8,128)S(1)} %get-tuple-element.15.mult), custom_call_target="tpu_custom_call" | custom-call | tf_op jit(solution)/shard_map/free_last/pallas_call | solution.py:445
  238.7 0.1 copy.10
  238.8 0.1 copy.9
  238.8 0.7 copy_bitcast_fusion
  (1 shorter events, 0.0 us)
Async XLA Ops:
  0.6 83.7 %copy-start = (f32[32,8192]{1,0:T(8,128)S(1)}, f32[32,8192]{1,0:T(8,128)}, u32[]{:S(2)}) copy-start(f32[32,8192]{1,0:T(8,128)} %bias.3) | copy-start | bytes 3145732
  1.5 0.8 copy-start.1
  2.3 0.8 copy-start.3
  3.0 81.3 %copy-start.2 = (s32[8192]{0:T(1024)S(1)}, s32[8192]{0:T(1024)}, u32[]{:S(2)}) copy-start(s32[8192]{0:T(1024)} %param.7) | copy-start | bytes 98308
